TPU v7x, 256 devices: a whole 4x4x8 slice. The times are simulated.
256 devices in a mesh: gx: 64 (over z_lo, x, y, core), ba: 4 (over z_hi).
Axes of the slice: x: 4, y: 4, z: 8 (z_hi: 4, z_lo: 2; z = z_hi * 2 + z_lo), core: 2. Of those that a mesh axis runs over, the one named last changes fastest.
Arguments:
- spectra: bfloat16 [4, 2, 256, 20, 3456], P('ba', None, 'gx'), may hold values from -6 to 6
- cotangent: bfloat16 [4, 2, 256, 20, 3456], P('ba', None, 'gx'), may hold values from -6 to 6
- weights: bfloat16 [3456, 19200], P('gx'), may hold values from -1 to 1
Outputs:
- output_spectra: bfloat16 [4, 2, 256, 20, 3456], P('ba', None, 'gx')
- input_grad: bfloat16 [4, 2, 256, 20, 3456], P('ba', None, 'gx')
- weight_grad: float32 [3456, 19200], P('gx')
All inputs are finite; a program needn't handle non-finite values.
Results may differ from a plain program's by a relative error of at most 0.0066.
Values may be sent and summed in bfloat16 or wider, within the bound.
A program may use at most 192 MiB of HBM per device.

v0:
```python
import math

import jax
import jax.numpy as jnp
from jax import lax
from jax.sharding import PartitionSpec as P

C = 20
X = 256
KX = 24


def build_table():
    mode_index = jnp.arange(KX, dtype=jnp.int32)
    wavenumber = jnp.where(mode_index < KX // 2, mode_index, mode_index - KX)
    positions = jnp.arange(X, dtype=jnp.int32)
    phases = wavenumber[:, None] * positions[None, :] % X
    angles = phases.astype(jnp.float32) * (2.0 * math.pi / X)
    factor = 1.0 / math.sqrt(X)
    cosine = jnp.cos(angles) * factor
    sine_part = jnp.sin(angles) * factor
    upper_rows = jnp.concatenate([cosine, sine_part], axis=1)
    lower_rows = jnp.concatenate([-sine_part, cosine], axis=1)
    return jnp.concatenate([upper_rows, lower_rows], axis=0).astype(jnp.bfloat16)


def invert(transform_rows, modes):
    batch, parts, kept, chans, local_modes = modes.shape
    flattened = modes.reshape(batch, parts * kept, chans * local_modes)
    result = jnp.einsum(
        "pq,bpn->bqn", transform_rows, flattened, preferred_element_type=jnp.float32
    )
    return result.reshape(batch, 2, X, chans, local_modes).astype(jnp.bfloat16)


def contract(coeffs, local_weights):
    real_part = jnp.einsum(
        "bkim,mkio->bkom", coeffs[:, 0], local_weights[:, 0], preferred_element_type=jnp.float32
    ) - jnp.einsum(
        "bkim,mkio->bkom", coeffs[:, 1], local_weights[:, 1], preferred_element_type=jnp.float32
    )
    imag_part = jnp.einsum(
        "bkim,mkio->bkom", coeffs[:, 0], local_weights[:, 1], preferred_element_type=jnp.float32
    ) + jnp.einsum(
        "bkim,mkio->bkom", coeffs[:, 1], local_weights[:, 0], preferred_element_type=jnp.float32
    )
    return jnp.stack([real_part, imag_part], axis=1)


def adjoint(grad_modes, local_weights):
    real_part = jnp.einsum(
        "bkom,mkio->bkim", grad_modes[:, 0], local_weights[:, 0], preferred_element_type=jnp.float32
    ) + jnp.einsum(
        "bkom,mkio->bkim", grad_modes[:, 1], local_weights[:, 1], preferred_element_type=jnp.float32
    )
    imag_part = jnp.einsum(
        "bkom,mkio->bkim", grad_modes[:, 1], local_weights[:, 0], preferred_element_type=jnp.float32
    ) - jnp.einsum(
        "bkom,mkio->bkim", grad_modes[:, 0], local_weights[:, 1], preferred_element_type=jnp.float32
    )
    return jnp.stack([real_part, imag_part], axis=1)


def outer_sum(coeffs, grad_modes):
    real_part = jnp.einsum(
        "bkim,bkom->mkio", coeffs[:, 0], grad_modes[:, 0], preferred_element_type=jnp.float32
    ) + jnp.einsum(
        "bkim,bkom->mkio", coeffs[:, 1], grad_modes[:, 1], preferred_element_type=jnp.float32
    )
    imag_part = jnp.einsum(
        "bkim,bkom->mkio", coeffs[:, 0], grad_modes[:, 1], preferred_element_type=jnp.float32
    ) - jnp.einsum(
        "bkim,bkom->mkio", coeffs[:, 1], grad_modes[:, 0], preferred_element_type=jnp.float32
    )
    stacked = jnp.stack([real_part, imag_part], axis=1)
    return stacked.reshape(stacked.shape[0], 2 * KX * C * C)


def on_device(spectra, cotangent, weights):
    transform_rows = build_table()
    local_weights = weights.reshape(weights.shape[0], 2, KX, C, C)

    def forward_fn(received):
        batch, parts, planes, chans, local_modes = received.shape
        flattened = received.reshape(batch, parts * planes, chans * local_modes)
        result = jnp.einsum(
            "pq,bqn->bpn", transform_rows, flattened, preferred_element_type=jnp.float32
        )
        return result.reshape(batch, 2, KX, chans, local_modes).astype(jnp.bfloat16)

    coeffs = forward_fn(lax.all_to_all(spectra, "gx", split_axis=4, concat_axis=2, tiled=True))
    mixed_modes = contract(coeffs, local_weights).astype(jnp.bfloat16)
    output = lax.all_to_all(
        invert(transform_rows, mixed_modes), "gx", split_axis=2, concat_axis=4, tiled=True
    )
    grad_modes = forward_fn(
        lax.all_to_all(cotangent, "gx", split_axis=4, concat_axis=2, tiled=True)
    )
    back_modes = adjoint(grad_modes, local_weights).astype(jnp.bfloat16)
    grad_in = lax.all_to_all(
        invert(transform_rows, back_modes), "gx", split_axis=2, concat_axis=4, tiled=True
    )
    weight_grad = lax.psum(outer_sum(coeffs, grad_modes), "ba")
    return (output, grad_in, weight_grad)


def solution(mesh):
    return jax.shard_map(
        on_device,
        mesh=mesh,
        in_specs=(P("ba", None, "gx", None, None), P("ba", None, "gx", None, None), P("gx", None)),
        out_specs=(P("ba", None, "gx", None, None), P("ba", None, "gx", None, None), P("gx", None)),
        check_vma=False,
    )
```

profile of v0, /device:TPU:8, one launch (start us, length us, event | category | flops | bytes accessed | tf_op | source)
XLA Modules:
  0.0 573.5 jit_solution(1410246709481791931)
XLA Ops:
  7.2 9.9 %copy.42 = bf16[1,2,4,20,3456]{3,2,1,0,4:T(4,128)(2,1)} copy(bf16[1,2,4,20,3456]{4,2,3,1,0:T(4,128)(2,1)} %param.4) | data formatting | bytes 2211840 | tf_op args[1]
  17.1 11.5 %reshape.212 = bf16[64,2,4320]{2,1,0:T(2,128)(2,1)} reshape(bf16[3456,1,2,4,20]{4,3,2,1,0:T(4,128)(2,1)} %bitcast.152) | data formatting | bytes 2211840
  28.5 9.3 %all-to-all-start.2 = ((bf16[64,2,4320]{2,1,0:T(2,128)(2,1)}), bf16[64,2,4320]{2,1,0:T(2,128)(2,1)S(1)}, u32[]{:S(2)}, u32[]{:S(2)}) async-start(bf16[64,2,4320]{2,1,0:T(2,128)(2,1)} %reshape.212), calls=%async_computation.2 | async-start | bytes 2228224 | tf_op jit(solution)/shard_map/all_to_all | solution.py:97
  37.8 7.9 %copy.35 = bf16[1,2,4,20,3456]{3,2,1,0,4:T(4,128)(2,1)} copy(bf16[1,2,4,20,3456]{4,2,3,1,0:T(4,128)(2,1)S(1)} %copy-done.4) | data formatting | bytes 2211840 | tf_op args[0]
  45.8 11.5 %reshape.208 = bf16[64,2,4320]{2,1,0:T(2,128)(2,1)} reshape(bf16[3456,1,2,4,20]{4,3,2,1,0:T(4,128)(2,1)} %bitcast.153) | data formatting | bytes 2211840
  57.3 9.8 %all-to-all-start = ((bf16[64,2,4320]{2,1,0:T(2,128)(2,1)}), bf16[64,2,4320]{2,1,0:T(2,128)(2,1)}, u32[]{:S(2)}, u32[]{:S(2)}) async-start(bf16[64,2,4320]{2,1,0:T(2,128)(2,1)} %reshape.208), calls=%async_computation | async-start | bytes 2228224 | tf_op jit(solution)/shard_map/all_to_all | solution.py:91
  67.1 4.1 copy.38
  71.2 9.1 %reshape.186 = bf16[54,2,24,20,20]{0,4,3,2,1:T(8,128)(2,1)} reshape(bf16[54,19200]{0,1:T(8,128)(2,1)} %copy.38) | data formatting | bytes 4147200 | tf_op jit(solution)/shard_map/reshape | solution.py:81
  80.5 9.9 %reshape.213 = bf16[3456,1,2,4,20]{4,3,2,1,0:T(4,128)(2,1)} reshape(bf16[64,2,4320]{2,1,0:T(2,128)(2,1)S(1)} %all-to-all-done.2) | data formatting | bytes 2211840
  90.4 10.3 %copy.108 = bf16[1,2,4,20,64,54]{5,3,2,4,1,0:T(8,128)(2,1)S(1)} copy(bf16[1,2,4,20,64,54]{3,2,1,5,4,0:T(4,128)(2,1)} %bitcast.150) | data formatting | bytes 2211840 | tf_op jit(solution)/shard_map/all_to_all | solution.py:97
  100.7 2.7 reshape.188
  103.4 1.6 fusion.11
  105.0 0.3 convert_element_type.127
  105.3 0.9 convert_bitcast_fusion.2
  106.2 15.2 %reshape.209 = bf16[3456,1,2,4,20]{4,3,2,1,0:T(4,128)(2,1)} reshape(bf16[64,2,4320]{2,1,0:T(2,128)(2,1)} %all-to-all-done) | data formatting | bytes 2211840
  121.4 10.3 %copy.106 = bf16[1,2,4,20,64,54]{5,3,2,4,1,0:T(8,128)(2,1)S(1)} copy(bf16[1,2,4,20,64,54]{3,2,1,5,4,0:T(4,128)(2,1)} %bitcast.151) | data formatting | bytes 2211840 | tf_op jit(solution)/shard_map/all_to_all | solution.py:91
  131.7 2.7 reshape.184
  134.4 1.6 fusion.10
  136.0 0.3 convert_element_type.117
  136.3 1.0 convert_bitcast_fusion.3
  137.3 7.9 %fusion.6 = (f32[24,54,20]{1,2,0:T(8,128)S(1)}, f32[24,54,20]{1,2,0:T(8,128)S(1)}, f32[24,54,20]{1,2,0:T(8,128)S(1)}, f32[24,54,20]{1,2,0:T(8,128)S(1)}) fusion(f32[24,54,20]{1,2,0:T(8,128)} %get-tuple-element.32, bf16[54,2,24,20,20]{0,4,3,2,1:T(8,128)(2,1)} %reshape.186, f32[24,54,20]{1,2,0:T(8,128)} %get-tuple-element.31), kind=kLoop, calls=%fused_computation.15 | loop fusion | flops 5080320 | bytes 2695680 | tf_op jit(solution)/shard_map/bkom,mkio->bkim/dot_general | solution.py:53
  145.4 0.2 convert_element_type.128
  145.6 0.5 fusion.9
  146.0 1.2 convert_element_type.132
  147.3 6.0 %copy.45 = bf16[1,2,256,20,54]{4,1,3,0,2:T(2,128)(2,1)S(1)} copy(bf16[1,2,256,20,54]{2,1,4,3,0:T(2,128)(2,1)} %convert_element_type.132) | data formatting | bytes 2211840 | tf_op jit(solution)/shard_map/convert_element_type | solution.py:33
  153.3 5.1 reshape.214
  158.5 9.1 %all-to-all-start.3 = ((bf16[64,2,4320]{2,1,0:T(2,128)(2,1)}), bf16[64,2,4320]{2,1,0:T(2,128)(2,1)}, u32[]{:S(2)}, u32[]{:S(2)}) async-start(bf16[64,2,4320]{2,1,0:T(2,128)(2,1)} %reshape.214), calls=%async_computation.3 | async-start | bytes 2228224 | tf_op jit(solution)/shard_map/all_to_all | solution.py:100
  167.6 4.8 add_bitcast_fusion
  172.4 8.3 %pad_maximum_fusion = f32[54,2,24,20,20]{0,4,3,2,1:T(8,128)} fusion(f32[54,1,24,20,20]{0,4,3,2,1:T(8,128)} %get-tuple-element.25, f32[54,1,24,20,20]{0,4,3,2,1:T(8,128)S(1)} %get-tuple-element.24), kind=kLoop, calls=%fused_computation | loop fusion | flops 1036800 | bytes 8294400 | tf_op jit(solution)/shard_map/stack | solution.py:75
  180.7 11.7 %reshape.191 = f32[54,19200]{0,1:T(8,128)} reshape(f32[54,2,24,20,20]{0,4,3,2,1:T(8,128)} %pad_maximum_fusion) | data formatting | bytes 8294400 | tf_op jit(solution)/shard_map/reshape | solution.py:76
  192.4 0.9 copy-done.2
  193.5 5.0 fusion.2
  198.8 0.5 fusion.8
  199.2 1.2 convert_element_type.122
  200.5 6.0 %copy.39 = bf16[1,2,256,20,54]{4,1,3,0,2:T(2,128)(2,1)S(1)} copy(bf16[1,2,256,20,54]{2,1,4,3,0:T(2,128)(2,1)} %convert_element_type.122) | data formatting | bytes 2211840 | tf_op jit(solution)/shard_map/convert_element_type | solution.py:33
  206.5 4.9 reshape.210
  211.5 9.5 %all-to-all-start.1 = ((bf16[64,2,4320]{2,1,0:T(2,128)(2,1)}), bf16[64,2,4320]{2,1,0:T(2,128)(2,1)}, u32[]{:S(2)}, u32[]{:S(2)}) async-start(bf16[64,2,4320]{2,1,0:T(2,128)(2,1)} %reshape.210), calls=%async_computation.1 | async-start | bytes 2228224 | tf_op jit(solution)/shard_map/all_to_all | solution.py:93
  220.9 11.2 %reshape.215 = bf16[256,1,20,2,54]{4,3,2,1,0:T(2,128)(2,1)S(1)} reshape(bf16[64,2,4320]{2,1,0:T(2,128)(2,1)} %all-to-all-done.3) | data formatting | bytes 2211840
  232.1 0.6 copy.46
  232.8 0.7 copy.47
  233.5 6.1 %all_to_all.61 = bf16[1,2,4,20,3456]{4,2,3,1,0:T(4,128)(2,1)} reshape(bf16[1,2,4,20,64,54]{5,4,2,3,1,0:T(8,128)(2,1)S(1)} %copy.47) | data formatting | bytes 2211840 | tf_op jit(solution)/shard_map/all_to_all | solution.py:100
  239.6 35.6 %all-to-all-done.1 = bf16[64,2,4320]{2,1,0:T(2,128)(2,1)} async-done(((bf16[64,2,4320]{2,1,0:T(2,128)(2,1)}), bf16[64,2,4320]{2,1,0:T(2,128)(2,1)}, u32[]{:S(2)}, u32[]{:S(2)}) %all-to-all-start.1) | async-done | bytes 1105952 | tf_op jit(solution)/shard_map/all_to_all | solution.py:93
  275.2 11.2 %reshape.211 = bf16[256,1,20,2,54]{4,3,2,1,0:T(2,128)(2,1)S(1)} reshape(bf16[64,2,4320]{2,1,0:T(2,128)(2,1)} %all-to-all-done.1) | data formatting | bytes 2211840
  286.4 0.6 copy.40
  287.0 0.7 copy.41
  287.7 6.4 %all_to_all.54 = bf16[1,2,4,20,3456]{4,2,3,1,0:T(4,128)(2,1)} reshape(bf16[1,2,4,20,64,54]{5,4,2,3,1,0:T(8,128)(2,1)S(1)} %copy.41) | data formatting | bytes 2211840 | tf_op jit(solution)/shard_map/all_to_all | solution.py:93
  294.1 263.7 %all-reduce.2.cloned.1.call-done = f32[54,19200]{0,1:T(8,128)} async-done(((f32[54,19200]{0,1:T(8,128)}), f32[54,19200]{0,1:T(8,128)}) %all-reduce.2.cloned.1.call-update) | async-done | bytes 4147216 | tf_op jit(solution)/shard_map/psum | solution.py:103
  557.8 8.6 %copy.48 = f32[54,19200]{1,0:T(8,128)} copy(f32[54,19200]{0,1:T(8,128)} %all-reduce.2.cloned.1.call-done) | data formatting | bytes 8294400
  (21 shorter events, 0.8 us)
Async XLA Ops:
  17.1 20.8 %copy-start.4 = (bf16[1,2,4,20,3456]{4,2,3,1,0:T(4,128)(2,1)S(1)}, bf16[1,2,4,20,3456]{4,2,3,1,0:T(4,128)(2,1)}, u32[]{:S(2)}) copy-start(bf16[1,2,4,20,3456]{4,2,3,1,0:T(4,128)(2,1)} %param.3) | copy-start | bytes 3317764
  28.5 28.8 %all-to-all-start.2 = ((bf16[64,2,4320]{2,1,0:T(2,128)(2,1)}), bf16[64,2,4320]{2,1,0:T(2,128)(2,1)S(1)}, u32[]{:S(2)}, u32[]{:S(2)}) async-start(bf16[64,2,4320]{2,1,0:T(2,128)(2,1)} %reshape.212), calls=%async_computation.2 | async-start | bytes 2228224 | tf_op jit(solution)/shard_map/all_to_all | solution.py:97
  45.8 21.3 %copy-start = (bf16[54,19200]{1,0:T(8,128)(2,1)S(1)}, bf16[54,19200]{1,0:T(8,128)(2,1)}, u32[]{:S(2)}) copy-start(bf16[54,19200]{1,0:T(8,128)(2,1)} %param.5) | copy-start | bytes 6220804
  57.3 48.9 %all-to-all-start = ((bf16[64,2,4320]{2,1,0:T(2,128)(2,1)}), bf16[64,2,4320]{2,1,0:T(2,128)(2,1)}, u32[]{:S(2)}, u32[]{:S(2)}) async-start(bf16[64,2,4320]{2,1,0:T(2,128)(2,1)} %reshape.208), calls=%async_computation | async-start | bytes 2228224 | tf_op jit(solution)/shard_map/all_to_all | solution.py:91
  147.3 20.3 %copy-start.1 = (f32[54,24,20]{0,2,1:T(8,128)S(1)}, f32[54,24,20]{0,2,1:T(8,128)}, u32[]{:S(2)}) copy-start(f32[54,24,20]{0,2,1:T(8,128)} %get-tuple-element.33) | copy-start | bytes 311044
  158.5 53.0 %all-to-all-start.3 = ((bf16[64,2,4320]{2,1,0:T(2,128)(2,1)}), bf16[64,2,4320]{2,1,0:T(2,128)(2,1)}, u32[]{:S(2)}, u32[]{:S(2)}) async-start(bf16[64,2,4320]{2,1,0:T(2,128)(2,1)} %reshape.214), calls=%async_computation.3 | async-start | bytes 2228224 | tf_op jit(solution)/shard_map/all_to_all | solution.py:100
  167.5 390.2 %all-reduce.2.cloned.1.call-start = ((), (), s32[]{:S(2)}) async-start(), calls=%async_computation.4 | async-start | bytes 19660800 | tf_op jit(solution)/shard_map/psum | solution.py:103
  192.4 1.0 copy-start.2
  192.4 1.0 copy-start.3
  211.5 63.7 %all-to-all-start.1 = ((bf16[64,2,4320]{2,1,0:T(2,128)(2,1)}), bf16[64,2,4320]{2,1,0:T(2,128)(2,1)}, u32[]{:S(2)}, u32[]{:S(2)}) async-start(bf16[64,2,4320]{2,1,0:T(2,128)(2,1)} %reshape.210), calls=%async_computation.1 | async-start | bytes 2228224 | tf_op jit(solution)/shard_map/all_to_all | solution.py:93
Sparse Core Ops, SparseCore 0:
  192.6 365.1 all-reduce.1
where the time goes:
time: 583 us; the launch traced here: 573 us
  waiting for transfers between devices  299 us (51%)
  local copies, waits for them, and re-layouts  190 us (33%)
  starting transfers between devices  37.6 us (6%)
  other arithmetic  28.4 us (5%)
  between operations  14.5 us (2%)
    psum x1, waiting for transfers between devices, on_device(): weight_grad = lax.psum(outer_sum(coeffs, grad_modes), 'ba')  264 us
    unnamed x22, local copies, waits for them, and re-layouts  112 us
    all_to_all x1, waiting for transfers between devices, on_device(): lax.all_to_all(invert(transform_rows, mixed_modes), 'gx', split_axis=2, c...  35.6 us
    convert_element_type x4, local copies, waits for them, and re-layouts, invert(): return result.reshape(batch, 2, X, chans, local_modes).astype(jnp.bfloat16)  14.6 us
    another operation x2, other arithmetic, outer_sum(): stacked = jnp.stack([real_part, imag_part], axis=1)  13.1 us
    reshape x1, local copies, waits for them, and re-layouts, outer_sum(): return stacked.reshape(stacked.shape[0], 2 * KX * C * C)  11.7 us
  transfers between devices with their start and end apart: 5, of which 2 were waited for; matrix products, arithmetic and copies ran while one was open for 22% of the time, Pallas kernels for 0%

commit v1 on v0

v1 whole, which is shorter than its diff:
```python
import functools
import math

import jax
import jax.numpy as jnp
import numpy as np
from jax import lax
from jax.experimental import pallas as pl
from jax.experimental.pallas import tpu as pltpu
from jax.sharding import PartitionSpec as P

C = 20
X = 256
KX = 24
SHARD = 54
MODES = 3456
TILES = MODES // 128
PLANE = 32
COLS = 1152
NT = COLS // 128
GROUP = 8
GN = GROUP * C * C
CHUNK = 640
MESH = pl.DeviceIdType.MESH


def table():
    mode = np.arange(KX)
    wave = np.where(mode < KX // 2, mode, mode - KX)
    phases = wave[:, None] * np.arange(X)[None, :] % X
    angles = phases.astype(np.float32) * np.float32(2.0 * math.pi / X)
    factor = np.float32(1.0 / math.sqrt(X))
    c = np.cos(angles) * factor
    s = np.sin(angles) * factor
    full = np.concatenate([np.concatenate([c, s], 1), np.concatenate([-s, c], 1)], 0)
    return full.astype(jnp.bfloat16).astype(np.float32)


@functools.cache
def constants():
    f = table().reshape(2, 3, GROUP, 2, 2, PLANE, 4)
    f = f.transpose(4, 1, 0, 2, 5, 3, 6)
    fb = np.zeros((2, 2, 48, PLANE, 2, 8), np.float32)
    for z in range(2):
        rows = f[z].reshape(48, PLANE, 8)
        fb[z, 0, :, :, z] = rows
        fb[z, 1, :, :, 1 - z] = rows
    fb = fb.reshape(2, 96, 512)
    n = np.arange(GN)
    kk, i, o = n // (C * C), n // C % C, n % C
    r = np.arange(C * GROUP)
    ei = ((r // GROUP)[:, None] == i[None]) & ((r % GROUP)[:, None] == kk[None])
    eo = ((r // GROUP)[:, None] == o[None]) & ((r % GROUP)[:, None] == kk[None])
    bf = lambda a: a.astype(jnp.bfloat16)
    return bf(fb), bf(fb.transpose(0, 2, 1)), bf(ei.astype(np.float32)), bf(eo.astype(np.float32))


def spot(c):
    return 54 * c // 128, 54 * c % 128


def kernel(
    x_hbm, ct_hbm, w_hbm, fb_hbm, fbt_hbm, ei_hbm, eo_hbm,
    out_hbm, gin_hbm, wg_hbm,
    xb, xf, w, fb, fbt, ei, eo, sbuf, rbuf, zs, zr, coef, lown, lall, bt, mm, wg, ob,
    load_sem, ssem, rsem, zssem, zrsem, bssem, brsem, out_sem,
):
    me = lax.axis_index("gx")
    ba = lax.axis_index("ba")
    z = me // PLANE
    q = me % PLANE
    qx, qy, qc = q // 8, q // 2 % 4, q % 2

    def peer(j):
        dest = (qx + j // 8) % 4 * 8 + (qy + j // 2 % 4) % 4 * 2 + (qc + j % 2) % 2
        return dest

    def load(i, src, dst):
        copy = pltpu.make_async_copy(src, dst, load_sem.at[i])
        copy.start()
        return copy

    loads = [
        load(0, x_hbm, xb.at[0]),
        load(1, ct_hbm, xb.at[1]),
        load(2, fb_hbm, fb),
        load(3, ei_hbm, ei),
        load(4, eo_hbm, eo),
        load(5, w_hbm, w),
        load(6, fbt_hbm, fbt),
    ]

    bar = pltpu.get_barrier_semaphore()

    def greet(j, carry):
        pl.semaphore_signal(bar, inc=1, device_id=(z * PLANE + peer(j), ba), device_id_type=MESH)
        return carry

    lax.fori_loop(1, PLANE, greet, 0)
    zpeer = ((1 - z) * PLANE + q, ba)
    pl.semaphore_signal(bar, inc=1, device_id=zpeer, device_id_type=MESH)
    for d in range(1, 4):
        pl.semaphore_signal(bar, inc=1, device_id=(me, (ba + d) % 4), device_id_type=MESH)

    lane = lax.broadcasted_iota(jnp.int32, (8, 128), 1)

    def widen(which):
        def tile(t, carry):
            cols = pl.ds(pl.multiple_of(t * 128, 128), 128)
            for r in range(8):
                xf[t, r * 24 : r * 24 + C, :] = xb[which, r, :, cols].astype(jnp.float32)
            return carry

        lax.fori_loop(0, TILES, tile, 0)

    def pack(dest, store):
        halves = []
        for h in range(2):
            lane0 = 54 * (PLANE * h + dest)
            t0 = lane0 // 128
            amt = lane0 % 128
            t1 = jnp.minimum(t0 + 1, TILES - 1)
            mask = lane >= amt
            tiles = [None] * NT
            for c in range(C):
                T, pos = spot(c)
                a = xf[t0, pl.ds(c, 8, stride=24), :]
                b = xf[t1, pl.ds(c, 8, stride=24), :]
                v = pltpu.roll(jnp.where(mask, a, b), (pos + 128 - amt) % 128, 1)
                tiles[T] = v if pos == 0 else jnp.where(lane >= pos, v, tiles[T])
                if pos + 54 > 128:
                    tiles[T + 1] = v
            halves.append(tiles)
        for T in range(NT):
            both = jnp.concatenate([halves[0][T], halves[1][T]], axis=0)
            store(T, both.astype(jnp.bfloat16))

    def send(phase, dest):
        pltpu.make_async_remote_copy(
            src_ref=sbuf.at[phase, dest],
            dst_ref=rbuf.at[phase, q],
            send_sem=ssem.at[phase],
            recv_sem=rsem.at[phase],
            device_id=(z * PLANE + dest, ba),
            device_id_type=MESH,
        ).start()

    def received(phase):
        part = rbuf.at[phase, pl.ds(0, PLANE - 1)]
        pltpu.make_async_copy(part, part, rsem.at[phase]).wait()

    def scatter(phase):
        def own(T, value):
            rbuf[phase, q, :, T * 128 : T * 128 + 128] = value

        pack(q, own)

        def step(j, carry):
            dest = peer(j)

            def put(T, value):
                sbuf[phase, dest, :, T * 128 : T * 128 + 128] = value

            pack(dest, put)
            send(phase, dest)
            return carry

        lax.fori_loop(1, PLANE, step, 0)

    def swap(slot):
        copy = pltpu.make_async_remote_copy(
            src_ref=zs.at[slot], dst_ref=zr.at[slot], send_sem=zssem.at[slot],
            recv_sem=zrsem.at[slot], device_id=zpeer, device_id_type=MESH,
        )
        copy.start()
        return copy

    def transform(phase):
        rows = rbuf[phase].reshape(512, COLS)
        part = jnp.dot(fb[z, 48:96], rows, preferred_element_type=jnp.float32)
        zs[phase] = part.astype(jnp.bfloat16)
        copy = swap(phase)
        mine = jnp.dot(fb[z, 0:48], rows, preferred_element_type=jnp.float32)
        copy.wait_recv()
        coef[phase, ba] = (mine + zr[phase].astype(jnp.float32)).astype(jnp.bfloat16)
        return copy

    def gather(phase):
        copies = []
        for d in range(1, 4):
            copy = pltpu.make_async_remote_copy(
                src_ref=coef.at[phase, ba], dst_ref=coef.at[phase, ba],
                send_sem=bssem.at[phase], recv_sem=brsem.at[phase],
                device_id=(me, (ba + d) % 4), device_id_type=MESH,
            )
            copy.start()

    def gathered(phase):
        part = coef.at[phase, pl.ds(0, 3)]
        pltpu.make_async_copy(part, part, brsem.at[phase]).wait()
        pltpu.make_async_copy(part, part, bssem.at[phase]).wait()

    def turn(phase, sample, put):
        for pair in range(3):
            tiles = [
                coef[phase, sample, 16 * pair : 16 * pair + 16, T * 128 : T * 128 + 128].astype(
                    jnp.float32
                )
                for T in range(NT)
            ]
            for p in range(2):
                for c in range(C):
                    T, pos = spot(c)
                    v = tiles[T][8 * p : 8 * p + 8]
                    if pos + 54 > 128:
                        v = jnp.where(lane >= pos, v, tiles[T + 1][8 * p : 8 * p + 8])
                    if pos:
                        v = pltpu.roll(v, 128 - pos, 1)
                    bt[8 * c : 8 * c + 8, :] = v
                put(pair, p, bt[...].T[0:64, :].astype(jnp.bfloat16))

    def mix(phase, slot):
        def put(g, p, value):
            lown[g, 64 * p : 64 * p + 64, :] = value

        turn(phase, ba, put)
        expand, reduce = (ei, eo) if phase == 0 else (eo, ei)
        sign = -1.0 if phase == 0 else 1.0
        for g in range(3):

            def chunk(j, total):
                n0 = pl.multiple_of(j * CHUNK, 128)
                cols = pl.ds(n0, CHUNK)
                wide = jnp.dot(lown[g], expand[:, cols], preferred_element_type=jnp.float32)
                ar, ai = wide[0:54], wide[64:118]
                wr = w[:, pl.ds(pl.multiple_of(n0 + g * GN, 128), CHUNK)].astype(jnp.float32)
                wi = w[:, pl.ds(pl.multiple_of(n0 + g * GN + 3 * GN, 128), CHUNK)].astype(
                    jnp.float32
                )
                if phase == 0:
                    tr, ti = ar * wr - ai * wi, ar * wi + ai * wr
                else:
                    tr, ti = wr * ar + wi * ai, wr * ai - wi * ar
                zero = jnp.zeros((10, CHUNK), jnp.float32)
                both = jnp.concatenate([tr, zero, ti, zero], axis=0).astype(jnp.bfloat16)
                return total + lax.dot_general(
                    both, reduce[:, cols], (((1,), (1,)), ((), ())),
                    preferred_element_type=jnp.float32,
                )

            mm[g] = lax.fori_loop(
                0, GN // CHUNK, chunk, jnp.zeros((128, C * GROUP), jnp.float32)
            )
            back = mm[g].T
            bt[...] = back
            halves = []
            for p in range(2):
                tiles = [None] * NT
                for c in range(C):
                    T, pos = spot(c)
                    v = bt[8 * c : 8 * c + 8, :]
                    shift = (pos + 64 * p) % 128
                    if shift:
                        v = pltpu.roll(v, shift, 1)
                    tiles[T] = v if pos == 0 else jnp.where(lane >= pos, v, tiles[T])
                    if pos + 54 > 128:
                        tiles[T + 1] = v
                halves.append(tiles)
            for T in range(NT):
                both = jnp.concatenate([halves[0][T], halves[1][T]], axis=0)
                zs[slot, 16 * g : 16 * g + 16, T * 128 : T * 128 + 128] = both.astype(jnp.bfloat16)
        return swap(slot)

    def invert(phase, slot, copy):
        copy.wait_recv()
        modes = jnp.concatenate([zs[slot], zr[slot]], axis=0)
        step = 128
        for b in range(512 // step):
            rows = jnp.dot(
                fbt[z, b * step : b * step + step, :], modes, preferred_element_type=jnp.float32
            )
            first = b * step // 16
            sbuf[phase, first : first + step // 16] = rows.astype(jnp.bfloat16).reshape(
                step // 16, 16, COLS
            )
        rbuf[phase, q] = sbuf[phase, q]

        def one(j, carry):
            send(phase, peer(j))
            return carry

        lax.fori_loop(1, PLANE, one, 0)

    def unpack(phase, slot, dst):
        for h in range(2):

            def one(source, carry):
                lane0 = 54 * (PLANE * h + source)
                t0 = lane0 // 128
                amt = lane0 % 128
                mask = lane >= amt
                tiles = [
                    rbuf[phase, source, :, T * 128 : T * 128 + 128].astype(jnp.float32)[
                        8 * h : 8 * h + 8
                    ]
                    for T in range(NT)
                ]
                for c in range(C):
                    T, pos = spot(c)
                    v = tiles[T]
                    if pos + 54 > 128:
                        v = jnp.where(lane >= pos, v, tiles[T + 1])
                    v = pltpu.roll(v, (amt + 128 - pos) % 128, 1)
                    rows = pl.ds(c, 8, stride=24)
                    xf[t0, rows, :] = jnp.where(mask, v, xf[t0, rows, :])
                    xf[t0 + 1, rows, :] = v
                return carry

            lax.fori_loop(0, PLANE, one, 0)

        def tile(t, carry):
            cols = pl.ds(pl.multiple_of(t * 128, 128), 128)
            for r in range(8):
                ob[slot, r, :, cols] = xf[t, r * 24 : r * 24 + C, :].astype(jnp.bfloat16)
            return carry

        lax.fori_loop(0, TILES, tile, 0)
        copy = pltpu.make_async_copy(ob.at[slot], dst, out_sem.at[slot])
        copy.start()
        return copy

    def outer():
        for phase in range(2):

            def sample(s, carry):
                def put(g, p, value):
                    lall[phase, g, pl.ds(pl.multiple_of(p * 256 + s * 64, 64), 64), :] = value

                turn(phase, s, put)
                return carry

            lax.fori_loop(0, 4, sample, 0)
        for g in range(3):

            def chunk(j, carry):
                n0 = pl.multiple_of(j * CHUNK, 128)
                cols = pl.ds(n0, CHUNK)
                a = jnp.dot(lall[0, g], ei[:, cols], preferred_element_type=jnp.float32)
                b = jnp.dot(lall[1, g], eo[:, cols], preferred_element_type=jnp.float32)
                re = im = None
                for s in range(4):
                    ar, ai = a[64 * s : 64 * s + 54], a[256 + 64 * s : 256 + 64 * s + 54]
                    br, bi = b[64 * s : 64 * s + 54], b[256 + 64 * s : 256 + 64 * s + 54]
                    r, i = ar * br + ai * bi, ar * bi - ai * br
                    re, im = (r, i) if s == 0 else (re + r, im + i)
                wg[:, pl.ds(pl.multiple_of(n0 + g * GN, 128), CHUNK)] = re
                wg[:, pl.ds(pl.multiple_of(n0 + g * GN + 3 * GN, 128), CHUNK)] = im
                return carry

            lax.fori_loop(0, GN // CHUNK, chunk, 0)
        copy = pltpu.make_async_copy(wg, wg_hbm, out_sem.at[2])
        copy.start()
        return copy

    loads[0].wait()
    widen(0)
    pl.semaphore_wait(bar, PLANE - 1 + 1 + 3)
    scatter(0)
    loads[1].wait()
    widen(1)
    scatter(1)
    for copy in loads[2:]:
        copy.wait()
    swaps = []
    received(0)
    swaps.append(transform(0))
    swaps.append(mix(0, 2))
    gather(0)
    invert(2, 2, swaps[-1])
    received(1)
    swaps.append(transform(1))
    swaps.append(mix(1, 3))
    gather(1)
    invert(3, 3, swaps[-1])
    received(2)
    done = [unpack(2, 0, out_hbm)]
    gathered(0)
    gathered(1)
    done.append(outer())
    received(3)
    done.append(unpack(3, 1, gin_hbm))
    for copy in swaps:
        copy.wait_send()
    for phase in range(4):
        part = sbuf.at[phase, pl.ds(0, PLANE - 1)]
        pltpu.make_async_copy(part, part, ssem.at[phase]).wait()
    for copy in done:
        copy.wait()


def on_device(spectra, cotangent, weights):
    fb, fbt, ei, eo = constants()
    bf, f32 = jnp.bfloat16, jnp.float32
    vm = pltpu.VMEM
    dma = pltpu.SemaphoreType.DMA
    out, gin, wg = pl.pallas_call(
        kernel,
        out_shape=[
            jax.ShapeDtypeStruct((8, C, MODES), bf),
            jax.ShapeDtypeStruct((8, C, MODES), bf),
            jax.ShapeDtypeStruct((SHARD, 6 * GN), f32),
        ],
        in_specs=[pl.BlockSpec(memory_space=pl.ANY)] * 7,
        out_specs=[pl.BlockSpec(memory_space=pl.ANY)] * 3,
        scratch_shapes=[
            vm((2, 8, C, MODES), bf),
            vm((TILES + 1, 192, 128), f32),
            vm((SHARD, 6 * GN), bf),
            vm((2, 96, 512), bf),
            vm((2, 512, 96), bf),
            vm((C * GROUP, GN), bf),
            vm((C * GROUP, GN), bf),
            vm((4, PLANE, 16, COLS), bf),
            vm((4, PLANE, 16, COLS), bf),
            vm((4, 48, COLS), bf),
            vm((4, 48, COLS), bf),
            vm((2, 4, 48, COLS), bf),
            vm((3, 128, C * GROUP), bf),
            vm((2, 3, 512, C * GROUP), bf),
            vm((C * GROUP, 128), f32),
            vm((3, 128, C * GROUP), f32),
            vm((SHARD, 6 * GN), f32),
            vm((2, 8, C, MODES), bf),
            dma((7,)),
            dma((4,)),
            dma((4,)),
            dma((4,)),
            dma((4,)),
            dma((2,)),
            dma((2,)),
            dma((3,)),
        ],
        compiler_params=pltpu.CompilerParams(
            collective_id=0, has_side_effects=True, vmem_limit_bytes=56 << 20
        ),
        name="spectral_block",
    )(
        spectra.reshape(8, C, MODES),
        cotangent.reshape(8, C, MODES),
        weights,
        jnp.asarray(fb),
        jnp.asarray(fbt),
        jnp.asarray(ei),
        jnp.asarray(eo),
    )
    shape = (1, 2, 4, C, MODES)
    return out.reshape(shape), gin.reshape(shape), wg


def solution(mesh):
    field = P("ba", None, "gx", None, None)
    return jax.shard_map(
        on_device,
        mesh=mesh,
        in_specs=(field, field, P("gx", None)),
        out_specs=(field, field, P("gx", None)),
        check_vma=False,
    )
```

time: 583 us -> 114 us (0.20); the launches traced: 573 us -> 114 us
  waiting for transfers between devices: 299 us -> 0 us
  local copies, waits for them, and re-layouts: 190 us -> 11.4 us
  Pallas kernels: 0 us -> 101 us
  starting transfers between devices: 37.6 us -> 0 us
  other arithmetic: 28.4 us -> 0 us
  between operations: 14.5 us -> 0.66 us
    psum x1 -> x0, waiting for transfers between devices: 264 us -> none  [on_device(): weight_grad = lax.psum(outer_sum(coeffs, grad_modes), 'ba')]
    pallas_call x0 -> x1, Pallas kernels: none -> 101 us  [on_device(): pl.pallas_call(kernel, out_shape=[jax.ShapeDtypeStruct((8, C, MODES), bf)...]
    unnamed x22 -> x9, local copies, waits for them, and re-layouts: 112 us -> 11.4 us
    all_to_all x4 -> x0, starting transfers between devices: 37.6 us -> none  [the longest x1 9.77 us: on_device(): lax.all_to_all(spectra, 'gx', split_axis=4, concat_axis=2, tiled=True)]
    all_to_all x8 -> x0, local copies, waits for them, and re-layouts: 35.6 us -> none  [the longest x1 10.3 us: on_device(): lax.all_to_all(cotangent, 'gx', split_axis=4, concat_axis=2, tiled=True)]
    all_to_all x4 -> x0, waiting for transfers between devices: 35.6 us -> none  [the longest x1 35.6 us: on_device(): lax.all_to_all(invert(transform_rows, mixed_modes), 'gx', split_axis=2, c...]
    reshape x2 -> x0, local copies, waits for them, and re-layouts: 20.8 us -> none  [the longest x1 11.7 us: outer_sum(): return stacked.reshape(stacked.shape[0], 2 * KX * C * C)]
    another operation x9 -> x0, other arithmetic: 15.5 us -> none  [the longest x2 13.1 us: outer_sum(): stacked = jnp.stack([real_part, imag_part], axis=1)]
  transfers between devices with their start and end apart: 5 -> 0, of which waited for: 2 -> 0; matrix products, arithmetic and copies ran while one was open for 22% -> 0% of each run, Pallas kernels for 0% -> 0%
where the time goes in v1:
time: 114 us
  Pallas kernels  101 us (89%)
  local copies, waits for them, and re-layouts  11.4 us (10%)
    pallas_call x1, Pallas kernels, on_device(): pl.pallas_call(kernel, out_shape=[jax.ShapeDtypeStruct((8, C, MODES), bf)...  101 us
    unnamed x9, local copies, waits for them, and re-layouts  11.4 us

profile of v1, /device:TPU:8, one launch (start us, length us, event | category | flops | bytes accessed | tf_op | source)
XLA Modules:
  0.0 113.6 jit_solution(11902371259790985157)
XLA Ops:
  0.6 0.0 copy-start.1
  0.6 2.5 %copy.10 = bf16[1,2,4,20,3456]{4,3,2,1,0:T(8,128)(2,1)} copy(bf16[1,2,4,20,3456]{4,2,3,1,0:T(4,128)(2,1)} %param.7) | data formatting | bytes 2211840 | tf_op args[0]
  3.2 0.0 copy-done.1
  3.2 1.2 %copy.11 = bf16[1,2,4,20,3456]{4,3,2,1,0:T(8,128)(2,1)} copy(bf16[1,2,4,20,3456]{4,2,3,1,0:T(4,128)(2,1)S(1)} %copy-done.1) | data formatting | bytes 2211840 | tf_op args[1]
  4.4 101.5 %spectral_block.1 = (bf16[8,20,3456]{2,1,0:T(8,128)(2,1)}, bf16[8,20,3456]{2,1,0:T(8,128)(2,1)}, f32[54,19200]{1,0:T(8,128)}) custom-call(bf16[8,20,3456]{2,1,0:T(8,128)(2,1)} %bitcast.4, bf16[8,20,3456]{2,1,0:T(8,128)(2,1)} %bitcast.5, bf16[54,19200]{1,0:T(8,128)(2,1)} %w_hbm.1, bf16[2,96,512]{2,1,0:T(8,128)(2,1)} %constant.8.clone.fb_hbm, ...), custom_call_target="tpu_custom_call" | custom-call | tf_op jit(solution)/shard_map/spectral_block/pallas_call | solution.py:406
  105.9 0.0 copy-start
  105.9 2.9 %copy.12 = bf16[1,2,4,20,3456]{4,2,3,1,0:T(4,128)(2,1)} copy(bf16[1,2,4,20,3456]{4,3,2,1,0:T(8,128)(2,1)} %bitcast.7) | data formatting | bytes 2211840
  108.8 2.7 %copy.13 = bf16[1,2,4,20,3456]{4,2,3,1,0:T(4,128)(2,1)} copy(bf16[1,2,4,20,3456]{4,3,2,1,0:T(8,128)(2,1)} %bitcast.6) | data formatting | bytes 2211840
  111.5 0.0 copy-done
  111.5 2.0 %copy.15 = f32[54,19200]{1,0:T(8,128)} copy(f32[54,19200]{1,0:T(8,128)S(1)} %copy-done) | data formatting | bytes 8294400
Async XLA Ops:
  0.6 2.5 %copy-start.1 = (bf16[1,2,4,20,3456]{4,2,3,1,0:T(4,128)(2,1)S(1)}, bf16[1,2,4,20,3456]{4,2,3,1,0:T(4,128)(2,1)}, u32[]{:S(2)}) copy-start(bf16[1,2,4,20,3456]{4,2,3,1,0:T(4,128)(2,1)} %param.8) | copy-start | bytes 3317764
  105.9 5.6 %copy-start = (f32[54,19200]{1,0:T(8,128)S(1)}, f32[54,19200]{1,0:T(8,128)}, u32[]{:S(2)}) copy-start(f32[54,19200]{1,0:T(8,128)} %get-tuple-element.17) | copy-start | bytes 12441604

commit v2 on v1

v2 whole, which is shorter than its diff:
```python
import functools
import math

import jax
import jax.numpy as jnp
import numpy as np
from jax import lax
from jax.experimental import pallas as pl
from jax.experimental.pallas import tpu as pltpu
from jax.sharding import PartitionSpec as P

C = 20
X = 256
KX = 24
SHARD = 54
MODES = 3456
TILES = MODES // 128
PLANE = 32
COLS = 1152
NT = COLS // 128
GROUP = 8
GN = GROUP * C * C
MESH = pl.DeviceIdType.MESH


def table():
    mode = np.arange(KX)
    wave = np.where(mode < KX // 2, mode, mode - KX)
    phases = wave[:, None] * np.arange(X)[None, :] % X
    angles = phases.astype(np.float32) * np.float32(2.0 * math.pi / X)
    factor = np.float32(1.0 / math.sqrt(X))
    c = np.cos(angles) * factor
    s = np.sin(angles) * factor
    full = np.concatenate([np.concatenate([c, s], 1), np.concatenate([-s, c], 1)], 0)
    return full.astype(jnp.bfloat16).astype(np.float32)


@functools.cache
def constants():
    f = table().reshape(2, 3, GROUP, 2, 2, PLANE, 4)
    f = f.transpose(4, 1, 0, 2, 5, 3, 6)
    fb = np.zeros((2, 2, 48, PLANE, 2, 8), np.float32)
    for z in range(2):
        rows = f[z].reshape(48, PLANE, 8)
        fb[z, 0, :, :, z] = rows
        fb[z, 1, :, :, 1 - z] = rows
    fb = fb.reshape(2, 96, 512)
    bf = lambda a: a.astype(jnp.bfloat16)
    return bf(fb), bf(fb.transpose(0, 2, 1))


def spot(c):
    return 54 * c // 128, 54 * c % 128


def kernel(
    x_hbm, ct_hbm, w_hbm, fb_hbm, fbt_hbm,
    out_hbm, gin_hbm, wg_hbm,
    xb, xs, w, fb, fbt, sbuf, rbuf, zs, zr, coef, vt, vp, vq, wt, mt, ga, gb, wgt, wg, ob,
    load_sem, ssem, rsem, zssem, zrsem, bssem, brsem, out_sem,
):
    me = lax.axis_index("gx")
    ba = lax.axis_index("ba")
    z = me // PLANE
    q = me % PLANE
    qx, qy, qc = q // 8, q // 2 % 4, q % 2

    def peer(j):
        i = j // 2
        return (qx + i) % 4 * 8 + (qy + i // 4 + i) % 4 * 2 + (qc + j) % 2

    def load(i, src, dst):
        copy = pltpu.make_async_copy(src, dst, load_sem.at[i])
        copy.start()
        return copy

    loads = [
        load(0, x_hbm, xb.at[0]),
        load(1, ct_hbm, xb.at[1]),
        load(2, fb_hbm, fb),
        load(3, w_hbm, w),
        load(4, fbt_hbm, fbt),
    ]

    bar = pltpu.get_barrier_semaphore()

    def greet(j, carry):
        pl.semaphore_signal(bar, inc=1, device_id=(z * PLANE + peer(j), ba), device_id_type=MESH)
        return carry

    lax.fori_loop(1, PLANE, greet, 0)
    zpeer = ((1 - z) * PLANE + q, ba)
    pl.semaphore_signal(bar, inc=1, device_id=zpeer, device_id_type=MESH)
    for d in range(1, 4):
        pl.semaphore_signal(bar, inc=1, device_id=(me, (ba + d) % 4), device_id_type=MESH)

    lane = lax.broadcasted_iota(jnp.int32, (8, 128), 1)
    lane16 = lax.broadcasted_iota(jnp.int16, (16, 128), 1)

    def rows8(which, c, cols):
        return jnp.concatenate(
            [xb[which, p, c, :, cols].astype(jnp.float32) for p in range(2)], axis=0
        )

    def arrange(which):
        def tile(t, carry):
            def cols(u):
                return pl.ds(pl.multiple_of(jnp.minimum(u, TILES - 1) * 128, 128), 128)

            for c in range(C):
                low = rows8(which, c, cols(t))
                high = jnp.where(
                    lane >= 64, rows8(which, c, cols(t + 13)), rows8(which, c, cols(t + 14))
                )
                both = jnp.concatenate([low, pltpu.roll(high, 64, 1)], axis=0)
                xs[t, 16 * c : 16 * c + 16, :] = both.astype(jnp.bfloat16)
            return carry

        lax.fori_loop(0, 14, tile, 0)

    def pack(dest, store):
        lane0 = 54 * dest
        t0 = lane0 // 128
        amt = lane0 % 128
        t1 = jnp.minimum(t0 + 1, 13)
        mask = lane16 >= amt.astype(jnp.int16)
        merged = jnp.concatenate(
            [
                jnp.where(mask, xs[t0, 16 * c : 16 * c + 16, :], xs[t1, 16 * c : 16 * c + 16, :])
                for c in range(C)
            ],
            axis=0,
        )
        merged = pltpu.roll(merged, (128 - amt) % 128, 1)
        tiles = [None] * NT
        for c in range(C):
            T, pos = spot(c)
            v = merged[16 * c : 16 * c + 16]
            if pos:
                v = pltpu.roll(v, pos, 1)
            tiles[T] = v if pos == 0 else jnp.where(lane16 >= pos, v, tiles[T])
            if pos + 54 > 128:
                tiles[T + 1] = v
        for T in range(NT):
            store(T, tiles[T])

    def send(phase, dest):
        pltpu.make_async_remote_copy(
            src_ref=sbuf.at[phase, dest],
            dst_ref=rbuf.at[phase, q],
            send_sem=ssem.at[phase],
            recv_sem=rsem.at[phase],
            device_id=(z * PLANE + dest, ba),
            device_id_type=MESH,
        ).start()

    def received(phase):
        part = rbuf.at[phase, pl.ds(0, PLANE - 1)]
        pltpu.make_async_copy(part, part, rsem.at[phase]).wait()

    def scatter(phase):
        def own(T, value):
            rbuf[phase, q, :, T * 128 : T * 128 + 128] = value

        pack(q, own)

        def step(j, carry):
            dest = peer(j)

            def put(T, value):
                sbuf[phase, dest, :, T * 128 : T * 128 + 128] = value

            pack(dest, put)
            send(phase, dest)
            return carry

        lax.fori_loop(1, PLANE, step, 0)

    def swap(slot, g):
        part = (slot, pl.ds(16 * g, 16))
        copy = pltpu.make_async_remote_copy(
            src_ref=zs.at[part], dst_ref=zr.at[part], send_sem=zssem.at[slot, g],
            recv_sem=zrsem.at[slot, g], device_id=zpeer, device_id_type=MESH,
        )
        copy.start()
        return copy

    def transform(phase):
        rows = rbuf[phase].reshape(512, COLS)
        part = jnp.dot(fb[z, 48:96], rows, preferred_element_type=jnp.float32)
        zs[phase] = part.astype(jnp.bfloat16)
        copies = [swap(phase, g) for g in range(3)]
        swaps.extend(copies)
        mine = jnp.dot(fb[z, 0:48], rows, preferred_element_type=jnp.float32)
        return copies, mine

    def turn(phase, copies, mine):
        for g in range(3):
            copies[g].wait_recv()
            got = zr[phase, 16 * g : 16 * g + 16].astype(jnp.float32)
            full = (mine[16 * g : 16 * g + 16] + got).astype(jnp.bfloat16).astype(jnp.float32)
            tiles = [full[:, T * 128 : T * 128 + 128] for T in range(NT)]
            for c in range(C):
                T, pos = spot(c)
                halves = []
                for p in range(2):
                    v = tiles[T][8 * p : 8 * p + 8]
                    if pos + 54 > 128:
                        v = jnp.where(lane >= pos, v, tiles[T + 1][8 * p : 8 * p + 8])
                    shift = (128 + 64 * p - pos) % 128
                    halves.append(pltpu.roll(v, shift, 1) if shift else v)
                v = jnp.where(lane < 64, halves[0], halves[1])
                turned = pltpu.roll(v, 64, 1)
                rows = pl.ds(8 * g * C + c, 8, stride=C)
                vt[rows, :] = v
                if phase == 0:
                    vp[rows, :] = jnp.where(lane < 64, v, -v)
                    vq[rows, :] = turned
                else:
                    vp[rows, :] = v
                    vq[rows, :] = jnp.where(lane < 64, turned, -turned)
        coef[phase, ba] = vt[...].astype(jnp.bfloat16)

    def gather(phase):
        for d in range(1, 4):
            pltpu.make_async_remote_copy(
                src_ref=coef.at[phase, ba], dst_ref=coef.at[phase, ba],
                send_sem=bssem.at[phase], recv_sem=brsem.at[phase],
                device_id=(me, (ba + d) % 4), device_id_type=MESH,
            ).start()

    def gathered(phase):
        part = coef.at[phase, pl.ds(0, 3)]
        pltpu.make_async_copy(part, part, brsem.at[phase]).wait()
        pltpu.make_async_copy(part, part, bssem.at[phase]).wait()

    def turn_weights():
        r = lax.broadcasted_iota(jnp.int32, (128, 128), 0)
        eye = (r == lax.broadcasted_iota(jnp.int32, (128, 128), 1)).astype(jnp.bfloat16)
        zero = jnp.zeros((10, 128), jnp.float32)

        def one(j, carry):
            n0 = pl.multiple_of(j * 128, 128)
            wr = w[:, pl.ds(n0, 128)].astype(jnp.float32)
            wi = w[:, pl.ds(pl.multiple_of(n0 + 3 * GN, 128), 128)].astype(jnp.float32)
            both = jnp.concatenate([wr, zero, wi, zero], axis=0).astype(jnp.bfloat16)
            wt[pl.ds(n0, 128), :] = lax.dot_general(
                eye, both, (((1,), (1,)), ((), ())), preferred_element_type=jnp.float32
            )
            return carry

        lax.fori_loop(0, 3 * GN // 128, one, 0, unroll=5)

    def mix(phase, slot):
        low = lax.broadcasted_iota(jnp.int32, (C, 128), 1) < 64
        for g in range(3):

            def one(kk, carry):
                k = 8 * g + kk
                base = pl.multiple_of(k * (C * C), 8)
                first = second = jnp.zeros((C, 128), jnp.float32)
                for j in range(C):
                    if phase == 0:
                        rows = wt[pl.ds(base + C * j, C), :]
                    else:
                        rows = wt[pl.ds(base + j, C, stride=C), :]
                    first = first + vp[pl.ds(k * C + j, 1), :] * rows
                    second = second + vq[pl.ds(k * C + j, 1), :] * rows
                first = first + pltpu.roll(first, 64, 1)
                second = second + pltpu.roll(second, 64, 1)
                mt[pl.ds(pl.multiple_of(24 * k, 8), C), :] = jnp.where(low, first, second)
                return carry

            lax.fori_loop(0, 8, one, 0)
            halves = [[None] * NT, [None] * NT]
            for c in range(C):
                T, pos = spot(c)
                v = mt[pl.ds(8 * g * 24 + c, 8, stride=24), :]
                for p in range(2):
                    shift = (pos + 64 * p) % 128
                    u = pltpu.roll(v, shift, 1) if shift else v
                    tiles = halves[p]
                    tiles[T] = u if pos == 0 else jnp.where(lane >= pos, u, tiles[T])
                    if pos + 54 > 128:
                        tiles[T + 1] = u
            for T in range(NT):
                both = jnp.concatenate([halves[0][T], halves[1][T]], axis=0)
                zs[slot, 16 * g : 16 * g + 16, T * 128 : T * 128 + 128] = both.astype(jnp.bfloat16)
            swaps.append(swap(slot, g))
        return swaps[-3:]

    def invert(phase, slot, copies):
        for copy in copies:
            copy.wait_recv()
        modes = jnp.concatenate([zs[slot], zr[slot]], axis=0)
        step = 128
        for b in range(512 // step):
            rows = jnp.dot(
                fbt[z, b * step : b * step + step, :], modes, preferred_element_type=jnp.float32
            )
            first = b * step // 16
            sbuf[phase, first : first + step // 16] = rows.astype(jnp.bfloat16).reshape(
                step // 16, 16, COLS
            )
        rbuf[phase, q] = sbuf[phase, q]

        def one(j, carry):
            send(phase, peer(j))
            return carry

        lax.fori_loop(1, PLANE, one, 0)

    def unpack(phase, slot, dst):
        def one(source, carry):
            lane0 = 54 * source
            t0 = lane0 // 128
            amt = lane0 % 128
            mask = lane16 >= amt.astype(jnp.int16)
            tiles = [rbuf[phase, source, :, T * 128 : T * 128 + 128] for T in range(NT)]
            pieces = []
            for c in range(C):
                T, pos = spot(c)
                v = tiles[T]
                if pos + 54 > 128:
                    v = jnp.where(lane16 >= pos, v, tiles[T + 1])
                pieces.append(pltpu.roll(v, 128 - pos, 1) if pos else v)
            merged = pltpu.roll(jnp.concatenate(pieces, axis=0), amt, 1)
            for c in range(C):
                rows = slice(16 * c, 16 * c + 16)
                v = merged[rows]
                xs[t0, rows, :] = jnp.where(mask, v, xs[t0, rows, :])
                xs[t0 + 1, rows, :] = v
            return carry

        lax.fori_loop(0, PLANE, one, 0)

        def put(t, c, value):
            cols = pl.ds(pl.multiple_of(t * 128, 128), 128)
            for p in range(2):
                ob[slot, p, c, :, cols] = value[4 * p : 4 * p + 4].astype(jnp.bfloat16)

        def tile(t, carry):
            for c in range(C):
                rows = slice(16 * c, 16 * c + 16)
                here = xs[t, rows, :].astype(jnp.float32)
                after = xs[t + 1, rows, :].astype(jnp.float32)
                put(t, c, here[0:8])
                high = jnp.where(lane >= 64, here[8:16], after[8:16])
                put(t + 14, c, pltpu.roll(high, 64, 1))
            return carry

        lax.fori_loop(0, 13, tile, 0)
        for c in range(C):
            rows = slice(16 * c, 16 * c + 16)
            high = pltpu.roll(xs[0, rows, :].astype(jnp.float32)[8:16], 64, 1)
            low = xs[13, rows, :].astype(jnp.float32)[0:8]
            put(13, c, jnp.where(lane < 64, low, high))
        copy = pltpu.make_async_copy(ob.at[slot], dst, out_sem.at[slot])
        copy.start()
        return copy

    def outer():
        low = lax.broadcasted_iota(jnp.int32, (24 * C, 128), 1) < 64
        for s in range(4):
            a = coef[0, s].astype(jnp.float32)
            turned = pltpu.roll(a, 64, 1)
            ga[s, 0] = jnp.where(low, a, turned)
            ga[s, 1] = jnp.where(low, turned, a)
            b = coef[1, s].astype(jnp.float32)
            turned = pltpu.roll(b, 64, 1)
            gb[s, 0] = b
            gb[s, 1] = jnp.where(low, turned, -turned)

        def one(k, carry):
            base = pl.multiple_of(k * (C * C), 8)
            right = [[gb[s, u, pl.ds(k * C, C), :] for u in range(2)] for s in range(4)]
            for i in range(C):
                total = None
                for s in range(4):
                    for u in range(2):
                        term = ga[s, u, pl.ds(k * C + i, 1), :] * right[s][u]
                        total = term if total is None else total + term
                wgt[pl.ds(base + C * i, C), :] = total
            return carry

        lax.fori_loop(0, KX, one, 0)

        def flip(j, carry):
            n0 = pl.multiple_of(j * 128, 128)
            both = wgt[pl.ds(n0, 128), :].T
            wg[:, pl.ds(n0, 128)] = both[0:54]
            wg[:, pl.ds(pl.multiple_of(n0 + 3 * GN, 128), 128)] = both[64:118]
            return carry

        lax.fori_loop(0, 3 * GN // 128, flip, 0, unroll=5)
        copy = pltpu.make_async_copy(wg, wg_hbm, out_sem.at[2])
        copy.start()
        return copy

    swaps = []
    loads[0].wait()
    arrange(0)
    pl.semaphore_wait(bar, PLANE - 1 + 1 + 3)
    scatter(0)
    loads[1].wait()
    arrange(1)
    scatter(1)
    for copy in loads[2:]:
        copy.wait()
    turn_weights()
    received(0)
    turn(0, *transform(0))
    back = mix(0, 2)
    received(1)
    front = transform(1)
    invert(2, 2, back)
    gather(0)
    turn(1, *front)
    back = mix(1, 3)
    gather(1)
    invert(3, 3, back)
    received(2)
    done = [unpack(2, 0, out_hbm)]
    gathered(0)
    gathered(1)
    done.append(outer())
    received(3)
    done.append(unpack(3, 1, gin_hbm))
    for copy in swaps:
        copy.wait_send()
    for phase in range(4):
        part = sbuf.at[phase, pl.ds(0, PLANE - 1)]
        pltpu.make_async_copy(part, part, ssem.at[phase]).wait()
    for copy in done:
        copy.wait()


def on_device(spectra, cotangent, weights):
    fb, fbt = constants()
    bf, f32 = jnp.bfloat16, jnp.float32
    vm = pltpu.VMEM
    dma = pltpu.SemaphoreType.DMA
    out, gin, wg = pl.pallas_call(
        kernel,
        out_shape=[
            jax.ShapeDtypeStruct((2, C, 4, MODES), bf),
            jax.ShapeDtypeStruct((2, C, 4, MODES), bf),
            jax.ShapeDtypeStruct((SHARD, 6 * GN), f32),
        ],
        in_specs=[pl.BlockSpec(memory_space=pl.ANY)] * 5,
        out_specs=[pl.BlockSpec(memory_space=pl.ANY)] * 3,
        scratch_shapes=[
            vm((2, 2, C, 4, MODES), bf),
            vm((15, 16 * C, 128), bf),
            vm((SHARD, 6 * GN), bf),
            vm((2, 96, 512), bf),
            vm((2, 512, 96), bf),
            vm((4, PLANE, 16, COLS), bf),
            vm((4, PLANE, 16, COLS), bf),
            vm((4, 48, COLS), bf),
            vm((4, 48, COLS), bf),
            vm((2, 4, KX * C, 128), bf),
            vm((KX * C, 128), f32),
            vm((KX * C, 128), f32),
            vm((KX * C, 128), f32),
            vm((3 * GN, 128), f32),
            vm((KX * 24, 128), f32),
            vm((4, 2, KX * C, 128), f32),
            vm((4, 2, KX * C, 128), f32),
            vm((3 * GN, 128), f32),
            vm((SHARD, 6 * GN), f32),
            vm((2, 2, C, 4, MODES), bf),
            dma((5,)),
            dma((4,)),
            dma((4,)),
            dma((4, 3)),
            dma((4, 3)),
            dma((2,)),
            dma((2,)),
            dma((3,)),
        ],
        compiler_params=pltpu.CompilerParams(
            collective_id=0, has_side_effects=True, vmem_limit_bytes=56 << 20
        ),
        name="spectral_block",
    )(
        spectra[0].swapaxes(1, 2),
        cotangent[0].swapaxes(1, 2),
        weights,
        jnp.asarray(fb),
        jnp.asarray(fbt),
    )
    return out.swapaxes(1, 2)[None], gin.swapaxes(1, 2)[None], wg


def solution(mesh):
    field = P("ba", None, "gx", None, None)
    return jax.shard_map(
        on_device,
        mesh=mesh,
        in_specs=(field, field, P("gx", None)),
        out_specs=(field, field, P("gx", None)),
        check_vma=False,
    )
```

time: 114 us -> 97.4 us (0.85)
  Pallas kernels: 101 us -> 87.8 us
  local copies, waits for them, and re-layouts: 11.4 us -> 7.43 us
    pallas_call x1, Pallas kernels: 101 us -> 87.8 us  [on_device(): pl.pallas_call(kernel, out_shape=[jax.ShapeDtypeStruct((2, C, 4, MODES),...]
    unnamed x9 -> x5, local copies, waits for them, and re-layouts: 11.4 us -> 7.43 us
where the time goes in v2:
time: 97.4 us; the launch traced here: 95.9 us
  Pallas kernels  87.8 us (90%)
  local copies, waits for them, and re-layouts  7.43 us (8%)
    pallas_call x1, Pallas kernels, on_device(): pl.pallas_call(kernel, out_shape=[jax.ShapeDtypeStruct((2, C, 4, MODES),...  87.8 us
    unnamed x5, local copies, waits for them, and re-layouts  7.43 us

profile of v2, /device:TPU:8, one launch (start us, length us, event | category | flops | bytes accessed | tf_op | source)
XLA Modules:
  0.0 95.9 jit_solution(2094849040049679268)
XLA Ops:
  0.6 87.8 %spectral_block.1 = (bf16[2,20,4,3456]{3,2,1,0:T(4,128)(2,1)}, bf16[2,20,4,3456]{3,2,1,0:T(4,128)(2,1)}, f32[54,19200]{1,0:T(8,128)}) custom-call(bf16[2,20,4,3456]{3,2,1,0:T(4,128)(2,1)} %bitcast.12, bf16[2,20,4,3456]{3,2,1,0:T(4,128)(2,1)} %bitcast.13, bf16[54,19200]{1,0:T(8,128)(2,1)} %w_hbm.1, bf16[2,96,512]{2,1,0:T(8,128)(2,1)} %constant.4.clone.fb_hbm, ...), custom_call_target="tpu_custom_call" | custom-call | tf_op jit(solution)/shard_map/spectral_block/pallas_call | solution.py:443
  88.4 0.0 copy-start
  88.4 2.8 %copy.11 = bf16[1,2,4,20,3456]{4,2,3,1,0:T(4,128)(2,1)} copy(bf16[1,2,4,20,3456]{4,2,3,1,0:T(4,128)(2,1)} %bitcast.15) | data formatting | bytes 2211840
  91.2 2.6 %copy.12 = bf16[1,2,4,20,3456]{4,2,3,1,0:T(4,128)(2,1)} copy(bf16[1,2,4,20,3456]{4,2,3,1,0:T(4,128)(2,1)} %bitcast.14) | data formatting | bytes 2211840
  93.8 0.0 copy-done
  93.8 2.0 %copy.13 = f32[54,19200]{1,0:T(8,128)} copy(f32[54,19200]{1,0:T(8,128)S(1)} %copy-done) | data formatting | bytes 8294400
Async XLA Ops:
  88.4 5.4 %copy-start = (f32[54,19200]{1,0:T(8,128)S(1)}, f32[54,19200]{1,0:T(8,128)}, u32[]{:S(2)}) copy-start(f32[54,19200]{1,0:T(8,128)} %get-tuple-element.14) | copy-start | bytes 12441604

commit v3 on v2

--- a/solution.py
+++ b/solution.py
@@ -332,7 +332,7 @@
                 xs[t0 + 1, rows, :] = v
             return carry
 
-        lax.fori_loop(0, PLANE, one, 0)
+        lax.fori_loop(0, PLANE, one, 0, unroll=4)
 
         def put(t, c, value):
             cols = pl.ds(pl.multiple_of(t * 128, 128), 128)
@@ -432,6 +432,26 @@
         part = sbuf.at[phase, pl.ds(0, PLANE - 1)]
         pltpu.make_async_copy(part, part, ssem.at[phase]).wait()
     for copy in done:
+        copy.wait()
+
+
+def hand_over(a, b, c, to_a, to_b, to_c, va, vb, vc, sem, sem_out):
+    parts = []
+    for first, rows in ((0, 16), (16, 16), (32, 16), (48, 6)):
+        parts.append((c, vc, to_c, (pl.ds(first, rows),)))
+    for src, mid, dst in ((a, va, to_a), (b, vb, to_b)):
+        for p in range(2):
+            parts.append((src, mid, dst, (p,)))
+    loads = []
+    for n, (src, mid, dst, part) in enumerate(parts):
+        loads.append(pltpu.make_async_copy(src.at[part], mid.at[part], sem.at[n]))
+        loads[-1].start()
+    stores = []
+    for n, (src, mid, dst, part) in enumerate(parts):
+        loads[n].wait()
+        stores.append(pltpu.make_async_copy(mid.at[part], dst.at[part], sem_out.at[n]))
+        stores[-1].start()
+    for copy in stores:
         copy.wait()
 
 
@@ -490,6 +510,15 @@
         jnp.asarray(fb),
         jnp.asarray(fbt),
     )
+    out, gin, wg = pl.pallas_call(
+        hand_over,
+        out_shape=[jax.ShapeDtypeStruct(v.shape, v.dtype) for v in (out, gin, wg)],
+        in_specs=[pl.BlockSpec(memory_space=pl.ANY)] * 3,
+        out_specs=[pl.BlockSpec(memory_space=pl.ANY)] * 3,
+        scratch_shapes=[vm(v.shape, v.dtype) for v in (out, gin, wg)] + [dma((8,)), dma((8,))],
+        compiler_params=pltpu.CompilerParams(vmem_limit_bytes=60 << 20),
+        name="hand_over",
+    )(out, gin, wg)
     return out.swapaxes(1, 2)[None], gin.swapaxes(1, 2)[None], wg
 
 

time: 97.4 us -> 92.4 us (0.949)
  local copies, waits for them, and re-layouts: 7.43 us -> 0 us
  Pallas kernels: 87.8 us -> 90.3 us
    unnamed x5 -> x0, local copies, waits for them, and re-layouts: 7.43 us -> none
    pallas_call x0 -> x1, Pallas kernels: none -> 5.36 us  [on_device(): pl.pallas_call(hand_over, out_shape=[jax.ShapeDtypeStruct(v.shape, v.dtyp...]
    pallas_call x1, Pallas kernels: 87.8 us -> 84.9 us  [on_device(): pl.pallas_call(kernel, out_shape=[jax.ShapeDtypeStruct((2, C, 4, MODES),...]
where the time goes in v3:
time: 92.4 us; the launch traced here: 90.9 us
  Pallas kernels  90.3 us (98%)
    pallas_call x1, Pallas kernels, on_device(): pl.pallas_call(kernel, out_shape=[jax.ShapeDtypeStruct((2, C, 4, MODES),...  84.9 us
    pallas_call x1, Pallas kernels, on_device(): pl.pallas_call(hand_over, out_shape=[jax.ShapeDtypeStruct(v.shape, v.dtyp...  5.36 us

profile of v3, /device:TPU:8, one launch (start us, length us, event | category | flops | bytes accessed | tf_op | source)
XLA Modules:
  0.0 90.9 jit_solution(7038064725099626077)
XLA Ops:
  0.6 84.9 %spectral_block.1 = (bf16[2,20,4,3456]{3,2,1,0:T(4,128)(2,1)}, bf16[2,20,4,3456]{3,2,1,0:T(4,128)(2,1)}, f32[54,19200]{1,0:T(8,128)}) custom-call(bf16[2,20,4,3456]{3,2,1,0:T(4,128)(2,1)} %bitcast.12, bf16[2,20,4,3456]{3,2,1,0:T(4,128)(2,1)} %bitcast.13, bf16[54,19200]{1,0:T(8,128)(2,1)} %w_hbm.1, bf16[2,96,512]{2,1,0:T(8,128)(2,1)} %constant.4.clone.fb_hbm, ...), custom_call_target="tpu_custom_call" | custom-call | tf_op jit(solution)/shard_map/spectral_block/pallas_call | solution.py:463
  85.6 5.4 %hand_over.1 = (bf16[2,20,4,3456]{3,2,1,0:T(4,128)(2,1)}, bf16[2,20,4,3456]{3,2,1,0:T(4,128)(2,1)}, f32[54,19200]{1,0:T(8,128)}) custom-call(bf16[2,20,4,3456]{3,2,1,0:T(4,128)(2,1)} %get-tuple-element.9.a, bf16[2,20,4,3456]{3,2,1,0:T(4,128)(2,1)} %get-tuple-element.10.b, f32[54,19200]{1,0:T(8,128)} %get-tuple-element.11.c), custom_call_target="tpu_custom_call" | custom-call | tf_op jit(solution)/shard_map/hand_over/pallas_call | solution.py:513

commit v4 on v3

--- a/solution.py
+++ b/solution.py
@@ -66,6 +66,7 @@
     qx, qy, qc = q // 8, q // 2 % 4, q % 2
 
     def peer(j):
+        j = 32 - j
         i = j // 2
         return (qx + i) % 4 * 8 + (qy + i // 4 + i) % 4 * 2 + (qc + j) % 2
 

time: 92.4 us -> 87.7 us (0.949)
  the two profiles are of different devices: /device:TPU:8 before, /device:TPU:1 now
where the time goes in v4:
time: 87.7 us; the launch traced here: 87.6 us
  Pallas kernels  87 us (99%)
    pallas_call x1, Pallas kernels, on_device(): pl.pallas_call(kernel, out_shape=[jax.ShapeDtypeStruct((2, C, 4, MODES),...  81.6 us
    pallas_call x1, Pallas kernels, on_device(): pl.pallas_call(hand_over, out_shape=[jax.ShapeDtypeStruct(v.shape, v.dtyp...  5.36 us

profile of v4, /device:TPU:1, one launch (start us, length us, event | category | flops | bytes accessed | tf_op | source)
XLA Modules:
  0.0 87.6 jit_solution(10962811097306562424)
XLA Ops:
  0.6 81.6 %spectral_block.1 = (bf16[2,20,4,3456]{3,2,1,0:T(4,128)(2,1)}, bf16[2,20,4,3456]{3,2,1,0:T(4,128)(2,1)}, f32[54,19200]{1,0:T(8,128)}) custom-call(bf16[2,20,4,3456]{3,2,1,0:T(4,128)(2,1)} %bitcast.12, bf16[2,20,4,3456]{3,2,1,0:T(4,128)(2,1)} %bitcast.13, bf16[54,19200]{1,0:T(8,128)(2,1)} %w_hbm.1, bf16[2,96,512]{2,1,0:T(8,128)(2,1)} %constant.4.clone.fb_hbm, ...), custom_call_target="tpu_custom_call" | custom-call | tf_op jit(solution)/shard_map/spectral_block/pallas_call | solution.py:464
  82.2 5.4 %hand_over.1 = (bf16[2,20,4,3456]{3,2,1,0:T(4,128)(2,1)}, bf16[2,20,4,3456]{3,2,1,0:T(4,128)(2,1)}, f32[54,19200]{1,0:T(8,128)}) custom-call(bf16[2,20,4,3456]{3,2,1,0:T(4,128)(2,1)} %get-tuple-element.9.a, bf16[2,20,4,3456]{3,2,1,0:T(4,128)(2,1)} %get-tuple-element.10.b, f32[54,19200]{1,0:T(8,128)} %get-tuple-element.11.c), custom_call_target="tpu_custom_call" | custom-call | tf_op jit(solution)/shard_map/hand_over/pallas_call | solution.py:514
